TPU v7x, 256 devices: a whole 4x4x8 slice. The times are simulated.
256 devices in a mesh: expert: 64 (over x, y_hi, z), tensor: 4 (over y_lo, core).
Axes of the slice: x: 4, y: 4 (y_hi: 2, y_lo: 2; y = y_hi * 2 + y_lo), z: 8, core: 2. Of those that a mesh axis runs over, the one named last changes fastest.
Arguments:
- tokens: bfloat16 [8192, 4096], P('expert', 'tensor'), may hold values from -6 to 6
- expert_ids: int32 [8192, 8], P('expert'), may hold values from 0 to 63, as said below
- slot_index: int32 [8192, 8], P('expert'), may hold values from -1 to 15, as said below
- gate_fixed: int32 [8192, 8], P('expert'), may hold values from 1024 to 32767
- gate_weight: bfloat16 [64, 4096, 1536], P('expert', None, 'tensor'), may hold values from -0.09375 to 0.09375
- up_weight: bfloat16 [64, 4096, 1536], P('expert', None, 'tensor'), may hold values from -0.09375 to 0.09375
- down_weight: bfloat16 [64, 1536, 4096], P('expert', 'tensor'), may hold values from -0.15625 to 0.15625
Outputs:
- moe_out: bfloat16 [8192, 4096], P('expert', 'tensor')
Inputs may be any that keep to these rules, and one draw needn't show every extreme that they name: `expert_ids`: each token names 8 different experts. One expert, drawn anew in every draw, is named by every token. `slot_index`: within each group of 128 consecutive tokens and each expert, the choices that name the expert, taken in a priority order of the group's tokens drawn anew in every draw, get slots 0, 1, 2 and so on; those past slot 15 get -1. No two choices of one group and expert share a slot. In every draw some expert fills all 16 slots in every group.
All inputs are finite; a program needn't handle non-finite values.
Results may differ from a plain program's by a relative error of at most 0.017.
Values may be sent and summed in bfloat16 or wider, within the bound.
A program may use at most 128 MiB of HBM per device.

v0:
```python
import jax
import jax.numpy as jnp
from jax import lax
from jax.sharding import PartitionSpec as P

CAP = 16


def expert_ffn(routed, gate_weight, up_weight, down_weight):
    sources, item_count, width = routed.shape
    flat_rows = routed.reshape(sources * item_count, width)
    gate_act = jnp.dot(flat_rows, gate_weight[0], preferred_element_type=jnp.float32)
    up_act = jnp.dot(flat_rows, up_weight[0], preferred_element_type=jnp.float32)
    hidden = (jax.nn.silu(gate_act) * up_act).astype(jnp.bfloat16)
    partial_value = jnp.dot(hidden, down_weight[0], preferred_element_type=jnp.float32)
    partial_value = partial_value.astype(jnp.bfloat16).reshape(sources, item_count, width)
    summed = lax.psum_scatter(partial_value, "tensor", scatter_dimension=2, tiled=True).astype(
        jnp.float32
    )
    return summed.astype(jnp.bfloat16)


def shards(tokens, expert_ids, slot_index, gate_fixed, gate_weight, up_weight, down_weight):
    experts = lax.axis_size("expert")
    tok_rows, top_count = expert_ids.shape
    kept = slot_index >= 0
    local_token = jnp.arange(tok_rows * top_count, dtype=jnp.int32) // top_count
    position = jnp.where(kept, expert_ids * CAP + slot_index, experts * CAP).reshape(-1)
    slot_owner = (
        jnp.full((experts * CAP,), -1, jnp.int32).at[position].set(local_token, mode="drop")
    )
    filled = slot_owner >= 0
    owner_safe = jnp.maximum(slot_owner, 0)
    gathered = lax.all_gather(tokens, "tensor", axis=1, tiled=True)
    picked = gathered[owner_safe]
    picked = jnp.where(filled[:, None], picked, jnp.zeros((), picked.dtype))
    outgoing = picked.reshape(experts, CAP, gathered.shape[1])
    results = expert_ffn(
        lax.all_to_all(outgoing, "expert", split_axis=0, concat_axis=0, tiled=True),
        gate_weight,
        up_weight,
        down_weight,
    )
    returned = lax.all_to_all(results, "expert", split_axis=0, concat_axis=0, tiled=True)
    flat_index = jnp.where(kept, expert_ids * CAP + slot_index, 0)
    combine_weight = jnp.where(kept, gate_fixed.astype(jnp.float32) / 32768.0, 0.0)
    flat_rows = returned.reshape(experts * CAP, returned.shape[2])
    picked = flat_rows[flat_index]
    mixed = jnp.einsum("tk,tkd->td", combine_weight, picked.astype(jnp.float32))
    return mixed.astype(jnp.bfloat16)


def solution(mesh):
    in_specs = (
        P("expert", "tensor"),
        P("expert", None),
        P("expert", None),
        P("expert", None),
        P("expert", None, "tensor"),
        P("expert", None, "tensor"),
        P("expert", "tensor", None),
    )
    out_specs = P("expert", "tensor")
    return jax.shard_map(shards, mesh=mesh, in_specs=in_specs, out_specs=out_specs, check_vma=False)
```

profile of v0, /device:TPU:8, one launch (start us, length us, event | category | flops | bytes accessed | tf_op | source)
XLA Modules:
  0.0 434.6 jit_solution(8439705426103668612)
XLA Ops:
  6.5 0.7 all-gather.2.cloned.1.call-update
  7.3 0.0 reduce-scatter.2.cloned.1.call-start
  7.3 0.9 compare_select_fusion.1
  8.2 0.1 copy.8
  8.3 0.1 reshape.48
  8.4 4.3 scatter_custom_fusion
  12.7 0.1 broadcast_in_dim.37
  12.8 21.9 %all-gather.2.cloned.1.call-done = bf16[128,4096]{1,0:T(8,128)(2,1)} async-done(((bf16[128,1024]{1,0:T(8,128)(2,1)}), bf16[128,4096]{1,0:T(8,128)(2,1)}) %all-gather.2.cloned.1.call-update) | async-done | bytes 1048592 | tf_op jit(solution)/shard_map/all_gather | solution.py:34
  34.8 16.5 %gather_fusion = bf16[1024,4096]{1,0:T(8,128)(2,1)} fusion(bf16[128,4096]{1,0:T(8,128)(2,1)} %all-gather.2.cloned.1.call-done, s32[1024]{0:T(1024)S(1)} %maximum_clamp_fusion), kind=kCustom, calls=%fused_computation | custom fusion | bytes 16781312 | tf_op jit(solution)/shard_map/gather | solution.py:35
  51.2 7.2 %broadcast_select_fusion = bf16[64,16,4096]{2,1,0:T(8,128)(2,1)} fusion(bf16[64,16,4096]{2,1,0:T(8,128)(2,1)} %bitcast.28, pred[64,16]{1,0:T(8,128)(4,1)S(1)} %broadcast_in_dim.37), kind=kLoop, calls=%fused_computation.3 | loop fusion | flops 4194304 | bytes 16778240 | tf_op jit(solution)/shard_map/jit(_where)/select_n | solution.py:36
  58.5 200.8 %all_to_all.10 = bf16[64,16,4096]{2,1,0:T(8,128)(2,1)S(1)} all-to-all(bf16[64,16,4096]{2,1,0:T(8,128)(2,1)} %broadcast_select_fusion), channel_id=1, replica_groups=mesh['expert'=64,'tensor'=4] {'expert'}, dimensions={0} | all-to-all | bytes 16777216 | tf_op jit(solution)/shard_map/all_to_all | solution.py:39
  259.3 4.5 %fusion.3 = f32[1024,384]{1,0:T(8,128)S(1)} fusion(bf16[1024,4096]{1,0:T(8,128)(2,1)S(1)} %bitcast.30, bf16[1,4096,384]{2,1,0:T(8,128)(2,1)S(1)} %copy-done.3), kind=kOutput, calls=%fused_computation.8 | convolution fusion | flops 3221225472 | bytes 13107200 | tf_op jit(solution)/shard_map/dot_general | solution.py:12
  263.8 4.6 %multiply_convert_fusion = bf16[1024,384]{1,0:T(8,128)(2,1)S(1)} fusion(f32[1024,384]{1,0:T(8,128)S(1)} %fusion.3, bf16[1024,4096]{1,0:T(8,128)(2,1)S(1)} %bitcast.31, bf16[1,4096,384]{2,1,0:T(8,128)(2,1)S(1)} %copy-done.4), kind=kOutput, calls=%fused_computation.12 | convolution fusion | flops 3223584768 | bytes 13893632 | tf_op jit(solution)/shard_map/dot_general | solution.py:13
  268.4 6.7 %convolution_convert_fusion = bf16[1024,4096]{1,0:T(8,128)(2,1)} fusion(bf16[1024,384]{1,0:T(8,128)(2,1)S(1)} %multiply_convert_fusion, bf16[1,384,4096]{2,1,0:T(8,128)(2,1)S(1)} %copy-done), kind=kOutput, calls=%fused_computation.4 | convolution fusion | flops 3225419776 | bytes 12320768 | tf_op jit(solution)/shard_map/dot_general | solution.py:15
  275.0 0.0 reduce-scatter.2.cloned.1.call-update
  275.1 75.2 %reduce-scatter.2.cloned.1.call-done = bf16[64,16,1024]{2,1,0:T(8,128)(2,1)} async-done(((bf16[64,16,4096]{2,1,0:T(8,128)(2,1)}), bf16[64,16,1024]{2,1,0:T(8,128)(2,1)}) %reduce-scatter.2.cloned.1.call-update) | async-done | bytes 2097168 | tf_op jit(solution)/shard_map/reduce_scatter | solution.py:17
  350.3 13.3 %all-to-all-start.1 = ((bf16[64,16,1024]{2,1,0:T(8,128)(2,1)}), bf16[64,16,1024]{2,1,0:T(8,128)(2,1)}, u32[]{:S(2)}, u32[]{:S(2)}) async-start(bf16[64,16,1024]{2,1,0:T(8,128)(2,1)} %reduce-scatter.2.cloned.1.call-done), calls=%async_computation.2 | async-start | bytes 4194304 | tf_op jit(solution)/shard_map/all_to_all | solution.py:44
  363.6 0.1 copy.9
  363.7 0.1 reshape.62
  363.8 0.1 copy.10
  364.0 52.9 %all-to-all-done.1 = bf16[64,16,1024]{2,1,0:T(8,128)(2,1)} async-done(((bf16[64,16,1024]{2,1,0:T(8,128)(2,1)}), bf16[64,16,1024]{2,1,0:T(8,128)(2,1)}, u32[]{:S(2)}, u32[]{:S(2)}) %all-to-all-start.1) | async-done | bytes 2097184 | tf_op jit(solution)/shard_map/all_to_all | solution.py:44
  416.9 7.9 %gather_fusion.1 = bf16[1024,1024]{1,0:T(8,128)(2,1)} fusion(bf16[1024,1024]{1,0:T(8,128)(2,1)} %bitcast.8, s32[1024]{0:T(1024)S(1)} %broadcast_clamp_fusion), kind=kCustom, calls=%fused_computation.1 | custom fusion | bytes 4198400 | tf_op jit(solution)/shard_map/gather | solution.py:48
  424.7 2.3 fusion.5
  427.0 0.8 copy.13
  (17 shorter events, 0.1 us)
Async XLA Ops:
  6.5 261.8 %copy-start = (bf16[1,384,4096]{2,1,0:T(8,128)(2,1)S(1)}, bf16[1,384,4096]{2,1,0:T(8,128)(2,1)}, u32[]{:S(2)}) copy-start(bf16[1,384,4096]{2,1,0:T(8,128)(2,1)} %param.13) | copy-start | bytes 9437188
  6.5 28.2 %all-gather.2.cloned.1.call-start = ((), (), s32[]{:S(2)}) async-start(), calls=%async_computation.3 | async-start | bytes 1310720 | tf_op jit(solution)/shard_map/all_gather | solution.py:34
  7.3 343.1 %reduce-scatter.2.cloned.1.call-start = ((), (), s32[]{:S(2)}) async-start(), calls=%async_computation.4 | async-start | bytes 10485760 | tf_op jit(solution)/shard_map/reduce_scatter | solution.py:17
  58.5 200.8 %copy-start.3 = (bf16[1,4096,384]{2,1,0:T(8,128)(2,1)S(1)}, bf16[1,4096,384]{2,1,0:T(8,128)(2,1)}, u32[]{:S(2)}) copy-start(bf16[1,4096,384]{2,1,0:T(8,128)(2,1)} %param.11) | copy-start | bytes 9437188
  259.3 4.5 %copy-start.4 = (bf16[1,4096,384]{2,1,0:T(8,128)(2,1)S(1)}, bf16[1,4096,384]{2,1,0:T(8,128)(2,1)}, u32[]{:S(2)}) copy-start(bf16[1,4096,384]{2,1,0:T(8,128)(2,1)} %param.12) | copy-start | bytes 9437188
  275.1 88.7 %copy-start.1 = (s32[128,8]{0,1:T(8,128)S(1)}, s32[128,8]{0,1:T(8,128)}, u32[]{:S(2)}) copy-start(s32[128,8]{0,1:T(8,128)} %param.9) | copy-start | bytes 12292
  275.1 88.7 %copy-start.2 = (s32[128,8]{0,1:T(8,128)S(1)}, s32[128,8]{0,1:T(8,128)}, u32[]{:S(2)}) copy-start(s32[128,8]{0,1:T(8,128)} %param.10) | copy-start | bytes 12292
  350.3 66.5 %all-to-all-start.1 = ((bf16[64,16,1024]{2,1,0:T(8,128)(2,1)}), bf16[64,16,1024]{2,1,0:T(8,128)(2,1)}, u32[]{:S(2)}, u32[]{:S(2)}) async-start(bf16[64,16,1024]{2,1,0:T(8,128)(2,1)} %reduce-scatter.2.cloned.1.call-done), calls=%async_computation.2 | async-start | bytes 4194304 | tf_op jit(solution)/shard_map/all_to_all | solution.py:44
Sparse Core Ops, SparseCore 0:
  9.2 25.5 all-gather.1
  275.2 75.1 reduce-scatter.1
where the time goes:
time: 435 us
  blocking collectives  201 us (46%)
  waiting for transfers between devices  151 us (35%)
  local copies, waits for them, and re-layouts  30 us (7%)
  matrix products  18 us (4%)
  between operations  13.5 us (3%)
  starting transfers between devices  13.3 us (3%)
  other arithmetic  8.16 us (2%)
    all_to_all x1, blocking collectives, shards(): lax.all_to_all(outgoing, 'expert', split_axis=0, concat_axis=0, tiled=True)  201 us
    reduce_scatter x1, waiting for transfers between devices, expert_ffn(): lax.psum_scatter(partial_value, 'tensor', scatter_dimension=2, tiled=True)  75.2 us
    all_to_all x1, waiting for transfers between devices, shards(): lax.all_to_all(results, 'expert', split_axis=0, concat_axis=0, tiled=True)  52.9 us
    all_gather x1, waiting for transfers between devices, shards(): gathered = lax.all_gather(tokens, 'tensor', axis=1, tiled=True)  21.9 us
    gather x1, local copies, waits for them, and re-layouts, shards(): picked = gathered[owner_safe]  16.5 us
    all_to_all x1, starting transfers between devices, shards(): lax.all_to_all(results, 'expert', split_axis=0, concat_axis=0, tiled=True)  13.3 us
  transfers between devices with their start and end apart: 3, of which 3 were waited for; matrix products, arithmetic and copies ran while one was open for 1% of the time, Pallas kernels for 0%

commit v1 on v0

v1 whole, which is shorter than its diff:
```python
import functools

import jax
import jax.numpy as jnp
from jax import lax
from jax.experimental import pallas as pl
from jax.experimental.pallas import tpu as pltpu
from jax.sharding import PartitionSpec as P

CAP = 16
MESH = pl.DeviceIdType.MESH
BF16 = jnp.bfloat16
F32 = jnp.float32


def kernel(
    nx,
    nz,
    order,
    tok_ref,
    meta_ref,
    gate_hbm,
    up_hbm,
    down_hbm,
    out_ref,
    w1,
    wd,
    metas,
    zb,
    sel,
    xb,
    acc,
    hid,
    po,
    cr,
    ts,
    tr,
    ys,
    rb,
    zs,
    zr,
    w_sem,
    meta_send,
    meta_recv,
    zb_send,
    zb_recv,
    sel_send,
    sel_recv,
    t_send,
    t_recv,
    c1_send,
    c1_recv,
    c2_send,
    c2_recv,
    ce_send,
    ce_recv,
    tt_send,
    tt_recv,
    r_send,
    r_recv,
    zr_send,
    zr_recv,
):
    expert = lax.axis_index("expert")
    tensor = lax.axis_index("tensor")
    z = lax.rem(expert, nz)
    yh = lax.rem(expert // nz, 2)
    x = expert // (2 * nz)
    c = lax.rem(tensor, 2)
    yl = tensor // 2
    half = nz // 2
    tok, width = tok_ref.shape
    hw = width // 2
    hidden = hid.shape[1]
    own_q = tensor
    far_q = (1 - yl) * 2 + c

    def at_z(d):
        return (expert - z + lax.rem(z + d + nz, nz), tensor)

    def at_plane(xx, rel):
        if rel == 0:
            return ((xx * 2 + yh) * nz + z, tensor)
        return ((xx * 2 + 1 - yh) * nz + z, (1 - yl) * 2 + c)

    t_peer = (expert, far_q)
    c_peer = (expert, yl * 2 + 1 - c)

    def blocks(s):
        if s == 0:
            return 0, 1
        if s == half:
            return nz - 1, 1
        return 2 * s - 1, 2

    def remote(src, dst, send, recv, dev):
        return pltpu.make_async_remote_copy(
            src_ref=src,
            dst_ref=dst,
            send_sem=send,
            recv_sem=recv,
            device_id=dev,
            device_id_type=MESH,
        )

    def wait_bytes(ref, sem):
        pltpu.make_async_copy(ref, ref, sem).wait()

    loads = []
    for q in range(4):
        rows = pl.ds(q * width, width)
        loads.append(
            pltpu.make_async_copy(
                gate_hbm.at[0, rows, :], w1.at[q, :, pl.ds(0, hidden)], w_sem.at[q]
            )
        )
        loads.append(
            pltpu.make_async_copy(
                up_hbm.at[0, rows, :], w1.at[q, :, pl.ds(hidden, hidden)], w_sem.at[4 + q]
            )
        )
        loads.append(
            pltpu.make_async_copy(down_hbm.at[0, :, rows], wd.at[q], w_sem.at[8 + q])
        )
    for load in loads:
        load.start()

    barrier = pltpu.get_barrier_semaphore()
    peers = [at_z(d) for d in range(1, nz)]
    peers += [at_plane(lax.rem(x + d, nx), 0) for d in range(1, nx)]
    peers += [at_plane(lax.rem(x + d, nx), 1) for d in range(nx)]
    peers += [t_peer, c_peer]
    for peer in peers:
        pl.semaphore_signal(barrier, inc=1, device_id=peer, device_id_type=MESH)
    pl.semaphore_wait(barrier, len(peers))

    ends = []

    for d in range(1, nz):
        remote(meta_ref, metas.at[d], meta_send, meta_recv, at_z(d)).start()
    ends.append(lambda: wait_bytes(metas.at[pl.ds(1, nz - 1)], meta_send))
    metas[0] = meta_ref[...]

    def z_copies(s):
        if s == half:
            f_src = tok_ref if s == 1 else zb.at[2 * s - 3]
            b_src = tok_ref if s == 1 else zb.at[2 * s - 2]
            lo, hi = pl.ds(0, hw), pl.ds(hw, hw)
            return (
                remote(f_src.at[:, lo], zb.at[nz - 1, :, lo], zb_send.at[s, 0], zb_recv.at[s, 0], at_z(1)),
                remote(b_src.at[:, hi], zb.at[nz - 1, :, hi], zb_send.at[s, 1], zb_recv.at[s, 1], at_z(-1)),
            )
        f_src = tok_ref if s == 1 else zb.at[2 * s - 3]
        b_src = tok_ref if s == 1 else zb.at[2 * s - 2]
        return (
            remote(f_src, zb.at[2 * s - 1], zb_send.at[s, 0], zb_recv.at[s, 0], at_z(1)),
            remote(b_src, zb.at[2 * s], zb_send.at[s, 1], zb_recv.at[s, 1], at_z(-1)),
        )

    def z_send(s):
        for copy in z_copies(s):
            copy.start()
            ends.append(copy.wait_send)

    z_send(1)

    def delta(b):
        if b == 0:
            return 0
        if b == nz - 1:
            return half
        return (b + 1) // 2 if b % 2 == 1 else nz - b // 2

    seat = 2 * nx * CAP
    per_rel = nx * CAP

    def seat_codes():
        j = lax.broadcasted_iota(jnp.int32, (seat, tok), 0)
        rel = j // per_rel
        rest = j - rel * per_rel
        xe = rest // CAP
        slot = rest - xe * CAP
        far = yh + rel - 2 * yh * rel
        return ((xe * 2 + far) * nz + z) * CAP + slot

    state = {"meta": False}

    def stage_a(s):
        first, count = blocks(s)
        if s > 0:
            for copy in z_copies(s):
                copy.wait_recv()
            if s < half:
                z_send(s + 1)
            if not state["meta"]:
                wait_bytes(metas.at[pl.ds(1, nz - 1)], meta_recv)
                state["meta"] = True
        code = seat_codes()
        for b in range(first, first + count):
            pick = jnp.zeros((seat, tok), F32)
            for k in range(8):
                pick = jnp.where(metas[delta(b), pl.ds(k, 1), :] == code, 1.0, pick)
            src = tok_ref[...] if b == 0 else zb[b]
            rows = jnp.dot(pick.astype(BF16), src, preferred_element_type=F32).astype(BF16)
            sel[0, b] = rows[:per_rel]
            sel[1, b] = rows[per_rel:]
        bl = pl.ds(first, count)
        mine = pl.ds(pl.multiple_of(x * CAP, CAP), CAP)
        pltpu.make_async_copy(
            sel.at[0, bl, mine, :], xb.at[own_q, 0, bl, mine, :], sel_recv.at[s, 0]
        ).start()
        for rel in range(2):
            for d in range(1 - rel, nx):
                xx = lax.rem(x + d, nx)
                theirs = pl.ds(pl.multiple_of(xx * CAP, CAP), CAP)
                remote(
                    sel.at[rel, bl, theirs, :],
                    xb.at[own_q, rel, bl, mine, :],
                    sel_send.at[s, rel],
                    sel_recv.at[s, rel],
                    at_plane(xx, rel),
                ).start()
        ends.append(
            lambda: wait_bytes(sel.at[0, bl, pl.ds(0, per_rel - CAP), :], sel_send.at[s, 0])
        )
        ends.append(lambda: wait_bytes(sel.at[1, bl], sel_send.at[s, 1]))

    def t_copies(s):
        bl = pl.ds(*blocks(s))
        out = []
        for rel in range(2):
            ref = xb.at[own_q if rel == 0 else far_q, rel, bl]
            out.append(remote(ref, ref, t_send.at[s, rel], t_recv.at[s, rel], t_peer))
        return out

    def c_copies(s, late):
        bl = pl.ds(*blocks(s))
        send, recv = (c2_send, c2_recv) if late else (c1_send, c1_recv)
        out = []
        for rel in range(2):
            ref = xb.at[own_q if (rel == 0) != late else far_q, rel, bl]
            out.append(remote(ref, ref, send.at[s, rel], recv.at[s, rel], c_peer))
        return out

    def start_all(copies):
        for copy in copies:
            copy.start()
            ends.append(copy.wait_send)

    def stage_b(s):
        bl = pl.ds(*blocks(s))
        t_list, c_list = t_copies(s), c_copies(s, False)
        for rel in range(2):
            wait_bytes(xb.at[own_q if rel == 0 else far_q, rel, bl], sel_recv.at[s, rel])
            start_all([t_list[rel], c_list[rel]])

    def stage_c(s):
        t_list, c_list = t_copies(s), c_copies(s, True)
        for rel in range(2):
            t_list[rel].wait_recv()
            start_all([c_list[rel]])

    def ce_copies(s):
        bl = pl.ds(*blocks(s))
        return [
            remote(
                po.at[2 * p + 1 - c, :, bl],
                cr.at[p, :, bl],
                ce_send.at[s, p],
                ce_recv.at[s, p],
                c_peer,
            )
            for p in range(2)
        ]

    loaded = {"w1": False, "wd": False}

    def stage_d(s):
        first, count = blocks(s)
        bl = pl.ds(first, count)
        rows = count * seat
        for late in (False, True):
            for copy in c_copies(s, late):
                copy.wait_recv()
        if not loaded["w1"]:
            loaded["w1"] = True
            for load in loads:
                load.wait()

        def up_step(q, carry):
            part = jnp.dot(
                xb[q, :, bl].reshape(rows, width), w1[q], preferred_element_type=F32
            )
            acc[pl.ds(0, rows), :] += part
            return carry

        acc[pl.ds(0, rows), :] = jnp.zeros((rows, 2 * hidden), F32)
        lax.fori_loop(0, 4, up_step, 0)
        gate = acc[pl.ds(0, rows), pl.ds(0, hidden)]
        up = acc[pl.ds(0, rows), pl.ds(hidden, hidden)]
        hid[pl.ds(0, rows), :] = (gate / (1.0 + jnp.exp(-gate)) * up).astype(BF16)

        def down_step(p, core):
            q = 2 * p + core
            part = jnp.dot(hid[pl.ds(0, rows), :], wd[q], preferred_element_type=F32)
            po[q, :, bl] = part.astype(BF16).reshape(2, count, per_rel, width)
            return core

        lax.fori_loop(0, 2, down_step, 1 - c)
        start_all(ce_copies(s))
        lax.fori_loop(0, 2, down_step, c)

    def tt_copies(s):
        bl = pl.ds(*blocks(s))
        return [
            remote(ts.at[rel, bl], tr.at[rel, bl], tt_send.at[s, rel], tt_recv.at[s, rel], t_peer)
            for rel in range(2)
        ]

    def stage_f(s):
        bl = pl.ds(*blocks(s))
        copies = tt_copies(s)
        for copy in ce_copies(s):
            copy.wait_recv()
        for rel in range(2):
            p = 1 - yl if rel == 0 else yl
            both = po[2 * p + c, rel, bl].astype(F32) + cr[p, rel, bl].astype(F32)
            ts[rel, bl] = both.astype(BF16)
            start_all([copies[rel]])

    def stage_g(s):
        bl = pl.ds(*blocks(s))
        copies = tt_copies(s)
        mine = pl.ds(pl.multiple_of(x * CAP, CAP), CAP)
        for rel in range(2):
            p = yl if rel == 0 else 1 - yl
            copies[rel].wait_recv()
            total = po[2 * p + c, rel, bl].astype(F32) + cr[p, rel, bl].astype(F32)
            ys[rel, bl] = (total + tr[rel, bl].astype(F32)).astype(BF16)
            if rel == 0:
                pltpu.make_async_copy(
                    ys.at[0, bl, mine, :], rb.at[0, bl, mine, :], r_recv.at[s, 0]
                ).start()
            for d in range(1 - rel, nx):
                xx = lax.rem(x + d, nx)
                theirs = pl.ds(pl.multiple_of(xx * CAP, CAP), CAP)
                remote(
                    ys.at[rel, bl, theirs, :],
                    rb.at[rel, bl, mine, :],
                    r_send.at[s, rel],
                    r_recv.at[s, rel],
                    at_plane(xx, rel),
                ).start()
        ends.append(
            lambda: wait_bytes(ys.at[0, bl, pl.ds(0, per_rel - CAP), :], r_send.at[s, 0])
        )
        ends.append(lambda: wait_bytes(ys.at[1, bl], r_send.at[s, 1]))

    def back_copies(s):
        if s == half:
            b = nz - 1
            lo, hi = pl.ds(0, hw), pl.ds(hw, hw)
            return (
                remote(zs.at[b, :, lo], zr.at[b, :, lo], zr_send.at[s, 0], zr_recv.at[s, 0], at_z(-1)),
                remote(zs.at[b, :, hi], zr.at[b, :, hi], zr_send.at[s, 1], zr_recv.at[s, 1], at_z(1)),
            )
        return (
            remote(zs.at[2 * s - 1], zr.at[2 * s - 1], zr_send.at[s, 0], zr_recv.at[s, 0], at_z(-1)),
            remote(zs.at[2 * s], zr.at[2 * s], zr_send.at[s, 1], zr_recv.at[s, 1], at_z(1)),
        )

    def stage_h(s):
        first, count = blocks(s)
        bl = pl.ds(first, count)
        for rel in range(2):
            wait_bytes(rb.at[rel, bl], r_recv.at[s, rel])
        code = seat_codes()
        arrived = back_copies(s + 1) if s < half else None
        copies = back_copies(s) if s > 0 else None
        sums = []
        for b in range(first, first + count):
            high = jnp.zeros((seat, tok), F32)
            low = jnp.zeros((seat, tok), F32)
            for k in range(8):
                hit = metas[delta(b), pl.ds(k, 1), :] == code
                weight = metas[delta(b), pl.ds(8 + k, 1), :]
                top = weight // 128
                high = jnp.where(hit, top.astype(F32) / 256.0, high)
                low = jnp.where(hit, (weight - top * 128).astype(F32) / 32768.0, low)
            rows = jnp.concatenate([rb[0, b], rb[1, b]], axis=0)
            dims = (((0,), (0,)), ((), ()))
            total = lax.dot_general(high.astype(BF16), rows, dims, preferred_element_type=F32)
            total += lax.dot_general(low.astype(BF16), rows, dims, preferred_element_type=F32)
            if s == 0:
                for i in range(2):
                    arrived[i].wait_recv()
                if half == 1:
                    total += zr[nz - 1].astype(F32)
                else:
                    total += zr[1].astype(F32) + zr[2].astype(F32)
                out_ref[...] = total.astype(BF16)
                return
            if s == half:
                zs[b] = total.astype(BF16)
                start_all(copies)
                return
            i = b - first
            arrived[i].wait_recv()
            if s == half - 1:
                lo, hi = pl.ds(0, hw), pl.ds(hw, hw)
                if i == 0:
                    zs[b, :, lo] = (total[:, :hw] + zr[nz - 1, :, lo].astype(F32)).astype(BF16)
                    zs[b, :, hi] = total[:, hw:].astype(BF16)
                else:
                    zs[b, :, lo] = total[:, :hw].astype(BF16)
                    zs[b, :, hi] = (total[:, hw:] + zr[nz - 1, :, hi].astype(F32)).astype(BF16)
            else:
                zs[b] = (total + zr[2 * (s + 1) - 1 + i].astype(F32)).astype(BF16)
            start_all([copies[i]])

    stages = {
        "A": stage_a,
        "B": stage_b,
        "C": stage_c,
        "D": stage_d,
        "F": stage_f,
        "G": stage_g,
        "H": stage_h,
    }
    for name, s in order:
        stages[name](s)
    for end in ends:
        end()


def make_order(half):
    order = [("A", 0), ("B", 0), ("A", 1), ("B", 1), ("C", 0), ("D", 0)]
    for s in range(2, half + 1):
        order += [("A", s), ("B", s), ("C", s - 1)]
        order += [("D", s - 1)]
    order += [("C", half)]
    order += [("F", half - 1), ("D", half), ("F", half)]
    order += [("F", s) for s in range(half - 2, -1, -1)]
    order += [("G", half - 1), ("G", half), ("H", half), ("H", half - 1)]
    for s in range(half - 2, -1, -1):
        order += [("G", s), ("H", s)]
    return order


def moe(nx, nz, tokens, meta, gate_weight, up_weight, down_weight):
    tok, width = tokens.shape
    hidden = gate_weight.shape[2]
    half = nz // 2
    chunks = half + 1
    per_rel = nx * CAP
    rows = 4 * per_rel
    dma = pltpu.SemaphoreType.DMA
    pairs = dma((chunks, 2))
    vmem = pl.BlockSpec(memory_space=pltpu.VMEM)
    hbm = pl.BlockSpec(memory_space=pl.ANY)
    scratch = [
        pltpu.VMEM((4, width, 2 * hidden), BF16),
        pltpu.VMEM((4, hidden, width), BF16),
        pltpu.VMEM((nz, 16, tok), jnp.int32),
        pltpu.VMEM((nz, tok, width), BF16),
        pltpu.VMEM((2, nz, per_rel, width), BF16),
        pltpu.VMEM((4, 2, nz, per_rel, width), BF16),
        pltpu.VMEM((rows, 2 * hidden), F32),
        pltpu.VMEM((rows, hidden), BF16),
        pltpu.VMEM((4, 2, nz, per_rel, width), BF16),
        pltpu.VMEM((2, 2, nz, per_rel, width), BF16),
        pltpu.VMEM((2, nz, per_rel, width), BF16),
        pltpu.VMEM((2, nz, per_rel, width), BF16),
        pltpu.VMEM((2, nz, per_rel, width), BF16),
        pltpu.VMEM((2, nz, per_rel, width), BF16),
        pltpu.VMEM((nz, tok, width), BF16),
        pltpu.VMEM((nz, tok, width), BF16),
        dma((12,)),
        dma,
        dma,
    ] + [pairs] * 18
    return pl.pallas_call(
        functools.partial(kernel, nx, nz, make_order(half)),
        out_shape=jax.ShapeDtypeStruct((tok, width), BF16),
        in_specs=[vmem, vmem, hbm, hbm, hbm],
        out_specs=vmem,
        scratch_shapes=scratch,
        compiler_params=pltpu.CompilerParams(
            collective_id=0,
            has_side_effects=True,
            vmem_limit_bytes=60 * 1024 * 1024,
        ),
    )(tokens, meta, gate_weight, up_weight, down_weight)


def shards(nx, nz, tokens, expert_ids, slot_index, gate_fixed, gate_weight, up_weight, down_weight):
    place = jnp.where(slot_index >= 0, expert_ids * CAP + slot_index, -1)
    meta = jnp.concatenate([place.T, gate_fixed.T], axis=0)
    return moe(nx, nz, tokens, meta, gate_weight, up_weight, down_weight)


def solution(mesh, nx=4, nz=8):
    in_specs = (
        P("expert", "tensor"),
        P("expert", None),
        P("expert", None),
        P("expert", None),
        P("expert", None, "tensor"),
        P("expert", None, "tensor"),
        P("expert", "tensor", None),
    )
    return jax.shard_map(
        functools.partial(shards, nx, nz),
        mesh=mesh,
        in_specs=in_specs,
        out_specs=P("expert", "tensor"),
        check_vma=False,
    )
```

time: 435 us -> 140 us (0.32)
  blocking collectives: 201 us -> 0 us
  waiting for transfers between devices: 151 us -> 0 us
  Pallas kernels: 0 us -> 136 us
  local copies, waits for them, and re-layouts: 30 us -> 1.67 us
  matrix products: 18 us -> 0 us
  between operations: 13.5 us -> 0.01 us
  starting transfers between devices: 13.3 us -> 0 us
  other arithmetic: 8.16 us -> 1.99 us
    all_to_all x1 -> x0, blocking collectives: 201 us -> none  [shards(): lax.all_to_all(outgoing, 'expert', split_axis=0, concat_axis=0, tiled=True)]
    pallas_call x0 -> x1, Pallas kernels: none -> 136 us  [moe(): pl.pallas_call(functools.partial(kernel, nx, nz, make_order(half)), out_s...]
    reduce_scatter x1 -> x0, waiting for transfers between devices: 75.2 us -> none  [expert_ffn(): lax.psum_scatter(partial_value, 'tensor', scatter_dimension=2, tiled=True)]
    all_to_all x1 -> x0, waiting for transfers between devices: 52.9 us -> none  [shards(): lax.all_to_all(results, 'expert', split_axis=0, concat_axis=0, tiled=True)]
    gather x2 -> x0, local copies, waits for them, and re-layouts: 24.3 us -> none  [the longest x1 16.5 us: shards(): picked = gathered[owner_safe]]
    all_gather x1 -> x0, waiting for transfers between devices: 21.9 us -> none  [shards(): gathered = lax.all_gather(tokens, 'tensor', axis=1, tiled=True)]
    dot_general x4 -> x0, matrix products: 18 us -> none  [the longest x1 6.68 us: expert_ffn(): jnp.dot(hidden, down_weight[0], preferred_element_type=jnp.float32)]
    all_to_all x1 -> x0, starting transfers between devices: 13.3 us -> none  [shards(): lax.all_to_all(results, 'expert', split_axis=0, concat_axis=0, tiled=True)]
  transfers between devices with their start and end apart: 3 -> 0, of which waited for: 3 -> 0; matrix products, arithmetic and copies ran while one was open for 1% -> 0% of each run, Pallas kernels for 0% -> 0%
where the time goes in v1:
time: 140 us; the launch traced here: 139 us
  Pallas kernels  136 us (97%)
  other arithmetic  1.99 us (1%)
  local copies, waits for them, and re-layouts  1.67 us (1%)
    pallas_call x1, Pallas kernels, moe(): pl.pallas_call(functools.partial(kernel, nx, nz, make_order(half)), out_s...  136 us

profile of v1, /device:TPU:8, one launch (start us, length us, event | category | flops | bytes accessed | tf_op | source)
XLA Modules:
  0.0 139.4 jit_solution(68783690988986974)
XLA Ops:
  0.0 0.7 select_bitcast_fusion
  0.7 1.3 pad_add_fusion.meta_ref
  2.0 135.8 %shard_map.73 = bf16[128,1024]{1,0:T(8,128)(2,1)} custom-call(bf16[128,1024]{1,0:T(8,128)(2,1)} %tok_ref.1, s32[16,128]{1,0:T(8,128)} %pad_add_fusion.meta_ref, bf16[1,4096,384]{2,1,0:T(8,128)(2,1)} %gate_hbm.1, bf16[1,4096,384]{2,1,0:T(8,128)(2,1)} %up_hbm.1, bf16[1,384,4096]{2,1,0:T(8,128)(2,1)} %down_hbm.1), custom_call_target="tpu_custom_call" | custom-call | tf_op jit(solution)/shard_map/pallas_call | solution.py:482
  137.8 1.7 %copy.9 = bf16[128,1024]{1,0:T(8,128)(2,1)} copy(bf16[128,1024]{1,0:T(8,128)(2,1)} %shard_map.73) | data formatting | bytes 524288

commit v2 on v1

v2 whole, which is shorter than its diff:
```python
import functools

import jax
import jax.numpy as jnp
from jax import lax
from jax.experimental import pallas as pl
from jax.experimental.pallas import tpu as pltpu
from jax.sharding import PartitionSpec as P

CAP = 16
MESH = pl.DeviceIdType.MESH
BF16 = jnp.bfloat16
F32 = jnp.float32


D_COUNT = 2
R_COUNT = 2
ORDERS = {
    4: [
        "B0ab A1a C0ab A1b",
        "B1a U0 V0 A2a",
        "B1b A2b C1a B2a",
        "C1b A3a B2b U1",
        "A3b V1 B3a C2a",
        "B3b C2b A4ab U2",
        "V2 B4a C3a B4b",
        "C3b U3 V3 C4ab",
        "F3ba U4 V4 F4ba",
        "F2ba F1ba F0ba G3ba",
        "G4ba H4ba H3ba G2ba",
        "H2ba G1b G1a H1b",
        "G0b H1a G0a H0ba",
    ],
    1: [
        "B0ab A1ab B1ab C0ab",
        "U0 V0 C1ab U1",
        "V1 F0ba F1ba G0ba",
        "G1ba H1ba H0ba",
    ],
    2: [
        "B0ab A1a C0ab A1b",
        "B1a U0 V0 A2a",
        "B1b A2b C1a B2a",
        "C1b B2b U1 V1",
        "C2ab F1ba U2 V2",
        "F2ba F0ba G1ba G2ba",
        "H2ba H1ba G0ba H0ba",
    ],
}


def kernel(
    nx,
    nz,
    d_early,
    r_early,
    d_count,
    r_count,
    order,
    tok_hbm,
    ids_ref,
    slot_ref,
    weight_ref,
    gate_hbm,
    up_hbm,
    down_hbm,
    out_ref,
    tokx,
    w1,
    wd,
    metas,
    pk,
    wt,
    zb,
    sel,
    xb,
    acc,
    hid,
    po,
    cr,
    ts,
    tr,
    ys,
    rb,
    zs,
    zr,
    last_out,
    last_in,
    w_sem,
    tok_sem,
    e_send,
    e_recv,
    last_send,
    last_recv,
    meta_send,
    meta_recv,
    zb_send,
    zb_recv,
    sel_send,
    sel_recv,
    sx_recv,
    cx_send,
    cx_recv,
    t_send,
    t_recv,
    c1_send,
    c1_recv,
    c2_send,
    c2_recv,
    ce_send,
    ce_recv,
    tt_send,
    tt_recv,
    r_send,
    r_recv,
    zr_send,
    zr_recv,
):
    expert = lax.axis_index("expert")
    tensor = lax.axis_index("tensor")
    z = lax.rem(expert, nz)
    yh = lax.rem(expert // nz, 2)
    x = expert // (2 * nz)
    c = lax.rem(tensor, 2)
    yl = tensor // 2
    half = nz // 2
    tok, width = tok_hbm.shape
    def split(count, early):
        full = width + early
        cuts = [full * i // (128 * count) * 128 for i in range(count)]
        whole = [pl.ds(a, b - a) for a, b in zip(cuts, cuts[1:] + [full])]
        owns = [pl.ds(a, b - a) for a, b in zip(cuts, cuts[1:] + [width])]
        starts = [early] + cuts[1:]
        lates = [pl.ds(a, b - a) for a, b in zip(starts, cuts[1:] + [width])]
        sent = [pl.ds(late.start - early, late.size) for late in lates]
        return whole, owns, lates, sent

    d_whole, d_owns, d_lates, _ = split(d_count, d_early)
    r_whole, r_owns, r_lates, r_sent = split(r_count, r_early)
    extra = pl.ds(width, d_early)
    head = pl.ds(0, d_early)
    r_extra = pl.ds(width, r_early)
    r_head = pl.ds(0, r_early)

    def side(piece, count):
        return piece * 2 // count

    hidden = hid.shape[1]
    own_q = tensor
    far_q = (1 - yl) * 2 + c

    def at_z(d):
        return (expert - z + lax.rem(z + d + nz, nz), tensor)

    def at_plane(xx, rel):
        if rel == 0:
            return ((xx * 2 + yh) * nz + z, tensor)
        return ((xx * 2 + 1 - yh) * nz + z, (1 - yl) * 2 + c)

    t_peer = (expert, far_q)
    c_peer = (expert, yl * 2 + 1 - c)

    def blocks(s):
        if s == 0:
            return 0, 1
        if s == half:
            return nz - 1, 1
        return 2 * s - 1, 2

    def remote(src, dst, send, recv, dev):
        return pltpu.make_async_remote_copy(
            src_ref=src,
            dst_ref=dst,
            send_sem=send,
            recv_sem=recv,
            device_id=dev,
            device_id_type=MESH,
        )

    def wait_bytes(ref, sem):
        pltpu.make_async_copy(ref, ref, sem).wait()

    tok_load = pltpu.make_async_copy(tok_hbm, tokx.at[:, pl.ds(0, width)], tok_sem)
    tok_load.start()
    loads = []
    for q in range(4):
        rows = pl.ds(q * width, width)
        loads.append(
            pltpu.make_async_copy(
                gate_hbm.at[0, rows, :], w1.at[q, :, pl.ds(0, hidden)], w_sem.at[q]
            )
        )
        loads.append(
            pltpu.make_async_copy(
                up_hbm.at[0, rows, :], w1.at[q, :, pl.ds(hidden, hidden)], w_sem.at[4 + q]
            )
        )
        loads.append(
            pltpu.make_async_copy(down_hbm.at[0, :, rows], wd.at[q], w_sem.at[8 + q])
        )
    for load in loads:
        load.start()

    barrier = pltpu.get_barrier_semaphore()
    peers = [at_z(d) for d in range(1, nz)]
    peers += [at_plane(lax.rem(x + d, nx), 0) for d in range(1, nx)]
    peers += [at_plane(lax.rem(x + d, nx), 1) for d in range(nx)]
    peers += [t_peer, c_peer]
    for peer in peers:
        pl.semaphore_signal(barrier, inc=1, device_id=peer, device_id_type=MESH)

    metas[0, pl.ds(0, 8), :] = jnp.where(
        slot_ref[...] >= 0, ids_ref[...] * CAP + slot_ref[...], -1
    )
    metas[0, pl.ds(8, 8), :] = weight_ref[...]

    def delta(b):
        if b == 0:
            return 0
        if b == nz - 1:
            return half
        return (b + 1) // 2 if b % 2 == 1 else nz - b // 2

    seat = 2 * nx * CAP
    per_rel = nx * CAP

    def seat_codes():
        j = lax.broadcasted_iota(jnp.int32, (seat, tok), 0)
        rel = j // per_rel
        rest = j - rel * per_rel
        xe = rest // CAP
        slot = rest - xe * CAP
        far = yh + rel - 2 * yh * rel
        return ((xe * 2 + far) * nz + z) * CAP + slot

    def z_copy(s, way, piece):
        src = tokx if s == 1 else zb.at[2 * s - 3 + way]
        dst = zb.at[nz - 1] if s == half else zb.at[2 * s - 1 + way]
        cols = d_whole[piece]
        i = 2 * s + way
        return remote(
            src.at[:, cols], dst.at[:, cols], zb_send, zb_recv.at[i, piece], at_z(1 - 2 * way)
        )

    def z_parts(s, piece):
        return [z_copy(s, way, piece) for way in range(2) if s < half or way == side(piece, d_count)]

    def z_send(s, piece):
        start_all(z_parts(s, piece))

    def start_all(copies):
        for copy in copies:
            copy.start()

    def routing(b):
        code = seat_codes()
        pick = jnp.zeros((seat, tok), F32)
        high = jnp.zeros((seat, tok), F32)
        low = jnp.zeros((seat, tok), F32)
        for k in range(8):
            hit = metas[delta(b), pl.ds(k, 1), :] == code
            weight = metas[delta(b), pl.ds(8 + k, 1), :]
            top = weight // 128
            pick = jnp.where(hit, 1.0, pick)
            high = jnp.where(hit, top.astype(F32) / 256.0, high)
            low = jnp.where(hit, (weight - top * 128).astype(F32) / 32768.0, low)
        pk[b] = pick.astype(BF16)
        wt[b, :, pl.ds(0, seat)] = high.T.astype(BF16)
        wt[b, :, pl.ds(seat, seat)] = low.T.astype(BF16)

    def pick_rows(b, cols):
        src = tokx[:, cols] if b == 0 else zb[b, :, cols]
        rows = jnp.dot(pk[b], src, preferred_element_type=F32).astype(BF16)
        sel[0, b, :, cols] = rows[:per_rel]
        sel[1, b, :, cols] = rows[per_rel:]

    mine = pl.ds(pl.multiple_of(x * CAP, CAP), CAP)

    def to_plane(s, cols, quarter, there, send, recv):
        bl = pl.ds(*blocks(s))
        pltpu.make_async_copy(
            sel.at[0, bl, mine, cols], xb.at[quarter, 0, bl, mine, there], recv(0)
        ).start()
        for rel in range(2):
            for d in range(1 - rel, nx):
                xx = lax.rem(x + d, nx)
                theirs = pl.ds(pl.multiple_of(xx * CAP, CAP), CAP)
                remote(
                    sel.at[rel, bl, theirs, cols],
                    xb.at[quarter, rel, bl, mine, there],
                    send(rel),
                    recv(rel),
                    at_plane(xx, rel),
                ).start()

    def send_piece(s, piece):
        cols = d_owns[piece]
        to_plane(
            s, cols, own_q, cols, lambda r: sel_send.at[r], lambda r: sel_recv.at[s, r, piece]
        )
        if piece == d_count - 1:
            to_plane(s, extra, far_q, head, lambda r: sel_send.at[r], lambda r: sx_recv.at[s, r])

    routing(0)
    tok_load.wait()
    pick_rows(0, d_whole[0])
    pl.semaphore_wait(barrier, len(peers))

    e_copy = remote(tokx.at[:, head], tokx.at[:, extra], e_send, e_recv, t_peer)
    start_all([e_copy])
    z_send(1, 0)
    send_piece(0, 0)
    for d in range(1, nz):
        remote(metas.at[0], metas.at[d], meta_send, meta_recv, at_z(d)).start()
    for piece in range(1, d_count):
        if piece == d_count - 1:
            e_copy.wait_recv()
        z_send(1, piece)
        pick_rows(0, d_whole[piece])
        send_piece(0, piece)

    state = {"meta": False}

    def stage_a(s, piece):
        first, count = blocks(s)
        for copy in z_parts(s, piece):
            copy.wait_recv()
        if s < half:
            z_send(s + 1, piece)
        if not state["meta"]:
            wait_bytes(metas.at[pl.ds(1, nz - 1)], meta_recv)
            state["meta"] = True
        for b in range(first, first + count):
            if piece == 0:
                routing(b)
            pick_rows(b, d_whole[piece])
        send_piece(s, piece)

    def t_copies(s, piece):
        bl = pl.ds(*blocks(s))
        out = []
        for rel in range(2):
            ref = xb.at[own_q if rel == 0 else far_q, rel, bl, :, d_lates[piece]]
            out.append(remote(ref, ref, t_send, t_recv.at[s, rel, piece], t_peer))
        return out

    def c_copies(s, piece, part):
        bl = pl.ds(*blocks(s))
        send, recv = ((c1_send, c1_recv), (cx_send, cx_recv), (c2_send, c2_recv))[part]
        cols = (d_owns[piece], head, d_lates[piece])[part]
        out = []
        for rel in range(2):
            ref = xb.at[own_q if (rel == 0) == (part == 0) else far_q, rel, bl, :, cols]
            i = (s, rel) if part == 1 else (s, rel, piece)
            out.append(remote(ref, ref, send, recv.at[i], c_peer))
        return out

    def stage_b(s, piece):
        bl = pl.ds(*blocks(s))
        t_list, c_list = t_copies(s, piece), c_copies(s, piece, 0)
        for rel in range(2):
            got = xb.at[own_q if rel == 0 else far_q, rel, bl, :, d_owns[piece]]
            wait_bytes(got, sel_recv.at[s, rel, piece])
            start_all([t_list[rel], c_list[rel]])
        if piece == d_count - 1:
            x_list = c_copies(s, piece, 1)
            for rel in range(2):
                got = xb.at[far_q if rel == 0 else own_q, rel, bl, :, head]
                wait_bytes(got, sx_recv.at[s, rel])
                start_all([x_list[rel]])

    def stage_c(s, piece):
        t_list, c_list = t_copies(s, piece), c_copies(s, piece, 2)
        for rel in range(2):
            t_list[rel].wait_recv()
            start_all([c_list[rel]])

    def ce_copies(s):
        bl = pl.ds(*blocks(s))
        return [
            remote(
                po.at[2 * p + 1 - c, :, bl],
                cr.at[p, :, bl],
                ce_send,
                ce_recv.at[s, p],
                c_peer,
            )
            for p in range(2)
        ]

    loaded = {"w1": False, "wd": False}

    def stage_u(s):
        first, count = blocks(s)
        bl = pl.ds(first, count)
        rows = count * seat
        for part in range(3):
            for piece in range(d_count):
                if part != 1 or piece == d_count - 1:
                    for copy in c_copies(s, piece, part):
                        copy.wait_recv()
        if not loaded["w1"]:
            loaded["w1"] = True
            for load in loads:
                load.wait()

        xs = jnp.concatenate([xb[q, :, bl].reshape(rows, width) for q in range(4)], axis=1)
        ws = jnp.concatenate([w1[q] for q in range(4)], axis=0)
        acc[pl.ds(0, rows), :] = jnp.dot(xs, ws, preferred_element_type=F32)
        gate = acc[pl.ds(0, rows), pl.ds(0, hidden)]
        up = acc[pl.ds(0, rows), pl.ds(hidden, hidden)]
        hid[pl.ds(0, rows), :] = (gate / (1.0 + jnp.exp(-gate)) * up).astype(BF16)

    def stage_v(s):
        first, count = blocks(s)
        bl = pl.ds(first, count)
        rows = count * seat

        copies = ce_copies(s)
        for core in (1 - c, c):
            for p in range(2):
                q = 2 * p + core
                part = jnp.dot(hid[pl.ds(0, rows), :], wd[q], preferred_element_type=F32)
                po[q, :, bl] = part.astype(BF16).reshape(2, count, per_rel, width)
                start_all(copies[p : p + 1])
            copies = []

    def tt_copies(s, piece):
        bl = pl.ds(*blocks(s))
        cols = r_sent[piece]
        return [
            remote(
                ts.at[rel, bl, :, cols],
                tr.at[rel, bl, :, cols],
                tt_send,
                tt_recv.at[s, rel, piece],
                t_peer,
            )
            for rel in range(2)
        ]

    def cores(p, rel, bl, cols):
        ours = po[2 * p + c, rel, bl, :, cols].astype(F32)
        return ours + cr[p, rel, bl, :, cols].astype(F32)

    def stage_f(s, piece):
        bl = pl.ds(*blocks(s))
        copies = tt_copies(s, piece)
        if piece == r_count - 1:
            for copy in ce_copies(s):
                copy.wait_recv()
        for rel in range(2):
            p = 1 - yl if rel == 0 else yl
            ts[rel, bl, :, r_sent[piece]] = cores(p, rel, bl, r_lates[piece]).astype(BF16)
            start_all([copies[rel]])

    def stage_g(s, piece):
        bl = pl.ds(*blocks(s))
        copies = tt_copies(s, piece)
        cols = r_whole[piece]
        for rel in range(2):
            p = yl if rel == 0 else 1 - yl
            if piece == 0:
                ys[rel, bl, :, r_head] = cores(p, rel, bl, r_head).astype(BF16)
            elif piece == r_count - 1:
                ys[rel, bl, :, r_extra] = cores(1 - p, rel, bl, r_head).astype(BF16)
            copies[rel].wait_recv()
            total = cores(p, rel, bl, r_lates[piece]) + tr[rel, bl, :, r_sent[piece]].astype(F32)
            ys[rel, bl, :, r_lates[piece]] = total.astype(BF16)
            if rel == 0:
                pltpu.make_async_copy(
                    ys.at[0, bl, mine, cols], rb.at[0, bl, mine, cols], r_recv.at[s, 0, piece]
                ).start()
            for d in range(1 - rel, nx):
                xx = lax.rem(x + d, nx)
                theirs = pl.ds(pl.multiple_of(xx * CAP, CAP), CAP)
                remote(
                    ys.at[rel, bl, theirs, cols],
                    rb.at[rel, bl, mine, cols],
                    r_send.at[rel],
                    r_recv.at[s, rel, piece],
                    at_plane(xx, rel),
                ).start()
    def back_copy(s, way, piece):
        b = nz - 1 if s == half else 2 * s - 1 + way
        cols = r_whole[piece]
        i = 2 * s + way
        return remote(
            zs.at[b, :, cols], zr.at[b, :, cols], zr_send, zr_recv.at[i, piece], at_z(2 * way - 1)
        )

    last = remote(last_out, last_in, last_send, last_recv, t_peer)

    def stage_h(s, piece):
        first, count = blocks(s)
        cols = r_whole[piece]
        for rel in range(2):
            wait_bytes(rb.at[rel, pl.ds(first, count), :, cols], r_recv.at[s, rel, piece])
        for b in range(first, first + count):
            near, far = rb[0, b, :, cols], rb[1, b, :, cols]
            rows = jnp.concatenate([near, far, near, far], axis=0)
            total = jnp.dot(wt[b], rows, preferred_element_type=F32)
            for way in range(2) if s == 0 else (b - first,):
                if s == half or (s + 1 == half and way != side(piece, r_count)):
                    continue
                back_copy(s + 1, way, piece).wait_recv()
                src = nz - 1 if s + 1 == half else 2 * s + 1 + way
                total += zr[src, :, cols].astype(F32)
            if s > 0:
                zs[b, :, cols] = total.astype(BF16)
                start_all([back_copy(s, side(piece, r_count) if s == half else b - first, piece)])
            elif piece == r_count - 1:
                mid = r_owns[piece].size
                last_out[...] = total[:, mid:].astype(BF16)
                start_all([last])
                out_ref[:, r_owns[piece]] = total[:, :mid].astype(BF16)
            elif piece > 0:
                out_ref[:, cols] = total.astype(BF16)
            else:
                out_ref[:, r_lates[0]] = total[:, r_early:].astype(BF16)
                last.wait_recv()
                out_ref[:, r_head] = (total[:, :r_early] + last_in[...].astype(F32)).astype(BF16)

    stages = {
        "A": stage_a,
        "B": stage_b,
        "C": stage_c,
        "U": stage_u,
        "V": stage_v,
        "F": stage_f,
        "G": stage_g,
        "H": stage_h,
    }
    for name, *step in order:
        stages[name](*step)
    some = pl.ds(0, per_rel - CAP)
    e_copy.wait_send()
    last.wait_send()
    wait_bytes(metas.at[pl.ds(1, nz - 1)], meta_send)
    wait_bytes(zb.at[pl.ds(0, nz - 1)], zb_send)
    wait_bytes(zs.at[pl.ds(0, nz - 1)], zr_send)
    for ref, sem in ((sel, sel_send), (ys, r_send)):
        wait_bytes(ref.at[0, :, some, :], sem.at[0])
        wait_bytes(ref.at[1], sem.at[1])
    late = xb.at[0, :, :, :, pl.ds(d_early, width - d_early)]
    wait_bytes(late, t_send)
    wait_bytes(late, c2_send)
    wait_bytes(ts, tt_send)
    wait_bytes(xb.at[0], c1_send)
    wait_bytes(xb.at[0, :, :, :, head], cx_send)
    wait_bytes(cr, ce_send)


def make_order(half):
    order = []
    for word in " ".join(ORDERS[half]).split():
        step = (word[0], int(word[1]))
        for piece in word[2:]:
            order.append(step + ("abcdef".index(piece),))
        if len(word) == 2:
            order.append(step)
    return order


def moe(nx, nz, d_early, r_early, tokens, ids, slots, weights, gate_weight, up_weight, down_weight):
    tok, width = tokens.shape
    hidden = gate_weight.shape[2]
    half = nz // 2
    chunks = half + 1
    per_rel = nx * CAP
    rows = 4 * per_rel
    dma = pltpu.SemaphoreType.DMA
    d_full, r_full = width + d_early, width + r_early
    vmem = pl.BlockSpec(memory_space=pltpu.VMEM)
    hbm = pl.BlockSpec(memory_space=pl.ANY)
    scratch = [
        pltpu.VMEM((tok, d_full), BF16),
        pltpu.VMEM((4, width, 2 * hidden), BF16),
        pltpu.VMEM((4, hidden, width), BF16),
        pltpu.VMEM((nz, 16, tok), jnp.int32),
        pltpu.VMEM((nz, 2 * per_rel, tok), BF16),
        pltpu.VMEM((nz, tok, 4 * per_rel), BF16),
        pltpu.VMEM((nz, tok, d_full), BF16),
        pltpu.VMEM((2, nz, per_rel, d_full), BF16),
        pltpu.VMEM((4, 2, nz, per_rel, width), BF16),
        pltpu.VMEM((rows, 2 * hidden), F32),
        pltpu.VMEM((rows, hidden), BF16),
        pltpu.VMEM((4, 2, nz, per_rel, width), BF16),
        pltpu.VMEM((2, 2, nz, per_rel, width), BF16),
        pltpu.VMEM((2, nz, per_rel, width - r_early), BF16),
        pltpu.VMEM((2, nz, per_rel, width - r_early), BF16),
        pltpu.VMEM((2, nz, per_rel, r_full), BF16),
        pltpu.VMEM((2, nz, per_rel, r_full), BF16),
        pltpu.VMEM((nz, tok, r_full), BF16),
        pltpu.VMEM((nz, tok, r_full), BF16),
        pltpu.VMEM((tok, r_early), BF16),
        pltpu.VMEM((tok, r_early), BF16),
        dma((12,)),
        dma,
        dma,
        dma,
        dma,
        dma,
        dma,
        dma,
        dma,
        dma((2 * chunks, D_COUNT)),
        dma((2,)),
        dma((chunks, 2, D_COUNT)),
        dma((chunks, 2)),
        dma,
        dma((chunks, 2)),
        dma,
        dma((chunks, 2, D_COUNT)),
        dma,
        dma((chunks, 2, D_COUNT)),
        dma,
        dma((chunks, 2, D_COUNT)),
        dma,
        dma((chunks, 2)),
        dma,
        dma((chunks, 2, R_COUNT)),
        dma((2,)),
        dma((chunks, 2, R_COUNT)),
        dma,
        dma((2 * chunks, R_COUNT)),
    ]
    return pl.pallas_call(
        functools.partial(kernel, nx, nz, d_early, r_early, D_COUNT, R_COUNT, make_order(half)),
        out_shape=pltpu.VMEM((tok, width), BF16),
        in_specs=[hbm, vmem, vmem, vmem, hbm, hbm, hbm],
        out_specs=vmem,
        scratch_shapes=scratch,
        compiler_params=pltpu.CompilerParams(
            collective_id=0,
            has_side_effects=True,
            vmem_limit_bytes=60 * 1024 * 1024,
        ),
    )(tokens, ids, slots, weights, gate_weight, up_weight, down_weight)


def shards(nx, nz, d_early, r_early, tokens, expert_ids, slot_index, gate_fixed, *expert_weights):
    routing = (expert_ids.T, slot_index.T, gate_fixed.T)
    return moe(nx, nz, d_early, r_early, tokens, *routing, *expert_weights)


def solution(mesh, nx=4, nz=8, d_early=128, r_early=256):
    in_specs = (
        P("expert", "tensor"),
        P("expert", None),
        P("expert", None),
        P("expert", None),
        P("expert", None, "tensor"),
        P("expert", None, "tensor"),
        P("expert", "tensor", None),
    )
    return jax.shard_map(
        functools.partial(shards, nx, nz, d_early, r_early),
        mesh=mesh,
        in_specs=in_specs,
        out_specs=P("expert", "tensor"),
        check_vma=False,
    )
```

time: 140 us -> 116 us (0.83)
  Pallas kernels: 136 us -> 116 us
  other arithmetic: 1.99 us -> 0 us
    pallas_call x1, Pallas kernels: 136 us -> 116 us  [moe(): pl.pallas_call(functools.partial(kernel, nx, nz, d_early, r_early, D_COUN...]
where the time goes in v2:
time: 116 us
  Pallas kernels  116 us (100%)
    pallas_call x1, Pallas kernels, moe(): pl.pallas_call(functools.partial(kernel, nx, nz, d_early, r_early, D_COUN...  116 us

profile of v2, /device:TPU:8, one launch (start us, length us, event | category | flops | bytes accessed | tf_op | source)
XLA Modules:
  0.0 116.4 jit_solution(15119992127330272404)
XLA Ops:
  0.0 115.7 %shard_map.73 = bf16[128,1024]{1,0:T(8,128)(2,1)S(1)} custom-call(bf16[128,1024]{1,0:T(8,128)(2,1)} %tok_hbm.1, s32[8,128]{1,0:T(8,128)} %bitcast.3, s32[8,128]{1,0:T(8,128)} %bitcast.4, s32[8,128]{1,0:T(8,128)} %bitcast.5, bf16[1,4096,384]{2,1,0:T(8,128)(2,1)} %gate_hbm.1, bf16[1,4096,384]{2,1,0:T(8,128)(2,1)} %up_hbm.1, bf16[1,384,4096]{2,1,0:T(8,128)(2,1)} %down_hbm.1), custom_call_target="tpu_custom_call" | custom-call | tf_op jit(solution)/shard_map/pallas_call | solution.py:628
  115.7 0.7 copy.9

commit v3 on v2

--- a/solution.py
+++ b/solution.py
@@ -14,7 +14,6 @@
 
 
 D_COUNT = 2
-R_COUNT = 2
 ORDERS = {
     4: [
         "B0ab A1a C0ab A1b",
@@ -25,26 +24,33 @@
         "B3b C2b A4ab U2",
         "V2 B4a C3a B4b",
         "C3b U3 V3 C4ab",
-        "F3ba U4 V4 F4ba",
-        "F2ba F1ba F0ba G3ba",
-        "G4ba H4ba H3ba G2ba",
-        "H2ba G1b G1a H1b",
-        "G0b H1a G0a H0ba",
+        "F3ba G3c U4 V4",
+        "F4ba G4c F2ba G2c",
+        "G3b G3a H4c G4b",
+        "G4a F1ba G1c H3c",
+        "H4b H4a H3b H3a",
+        "G2b G2a F0ba G0c",
+        "H2c H2b H2a G1b",
+        "H1c G1a H1b H1a",
+        "H0c G0b G0a H0b",
+        "H0a L0",
     ],
     1: [
         "B0ab A1ab B1ab C0ab",
         "U0 V0 C1ab U1",
-        "V1 F0ba F1ba G0ba",
-        "G1ba H1ba H0ba",
+        "V1 F0ba G0c F1ba",
+        "G1c G1ba H1cba G0ba",
+        "H0cba L0",
     ],
     2: [
         "B0ab A1a C0ab A1b",
         "B1a U0 V0 A2a",
         "B1b A2b C1a B2a",
         "C1b B2b U1 V1",
-        "C2ab F1ba U2 V2",
-        "F2ba F0ba G1ba G2ba",
-        "H2ba H1ba G0ba H0ba",
+        "C2ab F1ba G1c U2",
+        "V2 F2ba G2c F0ba",
+        "G0c G1ba G2ba H2cba",
+        "H1cba G0ba H0cba L0",
     ],
 }
 
@@ -55,7 +61,6 @@
     d_early,
     r_early,
     d_count,
-    r_count,
     order,
     tok_hbm,
     ids_ref,
@@ -132,14 +137,16 @@
         owns = [pl.ds(a, b - a) for a, b in zip(cuts, cuts[1:] + [width])]
         starts = [early] + cuts[1:]
         lates = [pl.ds(a, b - a) for a, b in zip(starts, cuts[1:] + [width])]
-        sent = [pl.ds(late.start - early, late.size) for late in lates]
-        return whole, owns, lates, sent
-
-    d_whole, d_owns, d_lates, _ = split(d_count, d_early)
-    r_whole, r_owns, r_lates, r_sent = split(r_count, r_early)
+        return whole, owns, lates
+
+    d_whole, d_owns, d_lates = split(d_count, d_early)
+    late = width - r_early
+    mid = late // 256 * 128
+    r_count = 3
+    r_whole = (pl.ds(0, mid), pl.ds(mid, late - mid), pl.ds(late, 2 * r_early))
+    r_lates = (pl.ds(r_early, mid), pl.ds(r_early + mid, late - mid))
     extra = pl.ds(width, d_early)
     head = pl.ds(0, d_early)
-    r_extra = pl.ds(width, r_early)
     r_head = pl.ds(0, r_early)
 
     def side(piece, count):
@@ -233,6 +240,9 @@
         far = yh + rel - 2 * yh * rel
         return ((xe * 2 + far) * nz + z) * CAP + slot
 
+    def meta_copy(d):
+        return remote(metas.at[0], metas.at[d], meta_send, meta_recv.at[d], at_z(d))
+
     def z_copy(s, way, piece):
         src = tokx if s == 1 else zb.at[2 * s - 3 + way]
         dst = zb.at[nz - 1] if s == half else zb.at[2 * s - 1 + way]
@@ -311,7 +321,7 @@
     z_send(1, 0)
     send_piece(0, 0)
     for d in range(1, nz):
-        remote(metas.at[0], metas.at[d], meta_send, meta_recv, at_z(d)).start()
+        meta_copy(d).start()
     for piece in range(1, d_count):
         if piece == d_count - 1:
             e_copy.wait_recv()
@@ -319,19 +329,15 @@
         pick_rows(0, d_whole[piece])
         send_piece(0, piece)
 
-    state = {"meta": False}
-
     def stage_a(s, piece):
         first, count = blocks(s)
         for copy in z_parts(s, piece):
             copy.wait_recv()
         if s < half:
             z_send(s + 1, piece)
-        if not state["meta"]:
-            wait_bytes(metas.at[pl.ds(1, nz - 1)], meta_recv)
-            state["meta"] = True
         for b in range(first, first + count):
             if piece == 0:
+                meta_copy(delta(b)).wait_recv()
                 routing(b)
             pick_rows(b, d_whole[piece])
         send_piece(s, piece)
@@ -427,7 +433,7 @@
 
     def tt_copies(s, piece):
         bl = pl.ds(*blocks(s))
-        cols = r_sent[piece]
+        cols = r_whole[piece]
         return [
             remote(
                 ts.at[rel, bl, :, cols],
@@ -446,27 +452,27 @@
     def stage_f(s, piece):
         bl = pl.ds(*blocks(s))
         copies = tt_copies(s, piece)
-        if piece == r_count - 1:
+        if piece == 1:
             for copy in ce_copies(s):
                 copy.wait_recv()
         for rel in range(2):
             p = 1 - yl if rel == 0 else yl
-            ts[rel, bl, :, r_sent[piece]] = cores(p, rel, bl, r_lates[piece]).astype(BF16)
+            ts[rel, bl, :, r_whole[piece]] = cores(p, rel, bl, r_lates[piece]).astype(BF16)
             start_all([copies[rel]])
 
     def stage_g(s, piece):
         bl = pl.ds(*blocks(s))
-        copies = tt_copies(s, piece)
+        copies = tt_copies(s, piece) if piece < 2 else None
         cols = r_whole[piece]
         for rel in range(2):
             p = yl if rel == 0 else 1 - yl
-            if piece == 0:
-                ys[rel, bl, :, r_head] = cores(p, rel, bl, r_head).astype(BF16)
-            elif piece == r_count - 1:
-                ys[rel, bl, :, r_extra] = cores(1 - p, rel, bl, r_head).astype(BF16)
-            copies[rel].wait_recv()
-            total = cores(p, rel, bl, r_lates[piece]) + tr[rel, bl, :, r_sent[piece]].astype(F32)
-            ys[rel, bl, :, r_lates[piece]] = total.astype(BF16)
+            if piece == 2:
+                ys[rel, bl, :, pl.ds(late, r_early)] = cores(p, rel, bl, r_head).astype(BF16)
+                ys[rel, bl, :, pl.ds(width, r_early)] = cores(1 - p, rel, bl, r_head).astype(BF16)
+            else:
+                copies[rel].wait_recv()
+                total = cores(p, rel, bl, r_lates[piece]) + tr[rel, bl, :, cols].astype(F32)
+                ys[rel, bl, :, cols] = total.astype(BF16)
             if rel == 0:
                 pltpu.make_async_copy(
                     ys.at[0, bl, mine, cols], rb.at[0, bl, mine, cols], r_recv.at[s, 0, piece]
@@ -509,17 +515,17 @@
             if s > 0:
                 zs[b, :, cols] = total.astype(BF16)
                 start_all([back_copy(s, side(piece, r_count) if s == half else b - first, piece)])
-            elif piece == r_count - 1:
-                mid = r_owns[piece].size
-                last_out[...] = total[:, mid:].astype(BF16)
+            elif piece == 2:
+                last_out[...] = total[:, r_early:].astype(BF16)
                 start_all([last])
-                out_ref[:, r_owns[piece]] = total[:, :mid].astype(BF16)
-            elif piece > 0:
-                out_ref[:, cols] = total.astype(BF16)
+                acc[pl.ds(0, tok), r_head] = total[:, :r_early]
             else:
-                out_ref[:, r_lates[0]] = total[:, r_early:].astype(BF16)
-                last.wait_recv()
-                out_ref[:, r_head] = (total[:, :r_early] + last_in[...].astype(F32)).astype(BF16)
+                out_ref[:, r_lates[piece]] = total.astype(BF16)
+
+    def stage_l(s):
+        last.wait_recv()
+        both = acc[pl.ds(0, tok), r_head] + last_in[...].astype(F32)
+        out_ref[:, r_head] = both.astype(BF16)
 
     stages = {
         "A": stage_a,
@@ -530,6 +536,7 @@
         "F": stage_f,
         "G": stage_g,
         "H": stage_h,
+        "L": stage_l,
     }
     for name, *step in order:
         stages[name](*step)
@@ -542,9 +549,9 @@
     for ref, sem in ((sel, sel_send), (ys, r_send)):
         wait_bytes(ref.at[0, :, some, :], sem.at[0])
         wait_bytes(ref.at[1], sem.at[1])
-    late = xb.at[0, :, :, :, pl.ds(d_early, width - d_early)]
-    wait_bytes(late, t_send)
-    wait_bytes(late, c2_send)
+    crossed = xb.at[0, :, :, :, pl.ds(d_early, width - d_early)]
+    wait_bytes(crossed, t_send)
+    wait_bytes(crossed, c2_send)
     wait_bytes(ts, tt_send)
     wait_bytes(xb.at[0], c1_send)
     wait_bytes(xb.at[0, :, :, :, head], cx_send)
@@ -602,7 +609,7 @@
         dma,
         dma,
         dma,
-        dma,
+        dma((nz,)),
         dma,
         dma((2 * chunks, D_COUNT)),
         dma((2,)),
@@ -619,14 +626,14 @@
         dma,
         dma((chunks, 2)),
         dma,
-        dma((chunks, 2, R_COUNT)),
+        dma((chunks, 2, 3)),
         dma((2,)),
-        dma((chunks, 2, R_COUNT)),
-        dma,
-        dma((2 * chunks, R_COUNT)),
+        dma((chunks, 2, 3)),
+        dma,
+        dma((2 * chunks, 3)),
     ]
     return pl.pallas_call(
-        functools.partial(kernel, nx, nz, d_early, r_early, D_COUNT, R_COUNT, make_order(half)),
+        functools.partial(kernel, nx, nz, d_early, r_early, D_COUNT, make_order(half)),
         out_shape=pltpu.VMEM((tok, width), BF16),
         in_specs=[hbm, vmem, vmem, vmem, hbm, hbm, hbm],
         out_specs=vmem,

time: 116 us -> 110 us (0.948)
  Pallas kernels: 116 us -> 109 us
    pallas_call x1, Pallas kernels: 116 us -> 109 us  [moe(): pl.pallas_call(functools.partial(kernel, nx, nz, d_early, r_early, D_COUN...]
where the time goes in v3:
time: 110 us
  Pallas kernels  109 us (99%)
    pallas_call x1, Pallas kernels, moe(): pl.pallas_call(functools.partial(kernel, nx, nz, d_early, r_early, D_COUN...  109 us

profile of v3, /device:TPU:8, one launch (start us, length us, event | category | flops | bytes accessed | tf_op | source)
XLA Modules:
  0.0 110.1 jit_solution(2743746261356215817)
XLA Ops:
  0.0 109.4 %shard_map.73 = bf16[128,1024]{1,0:T(8,128)(2,1)S(1)} custom-call(bf16[128,1024]{1,0:T(8,128)(2,1)} %tok_hbm.1, s32[8,128]{1,0:T(8,128)} %bitcast.3, s32[8,128]{1,0:T(8,128)} %bitcast.4, s32[8,128]{1,0:T(8,128)} %bitcast.5, bf16[1,4096,384]{2,1,0:T(8,128)(2,1)} %gate_hbm.1, bf16[1,4096,384]{2,1,0:T(8,128)(2,1)} %up_hbm.1, bf16[1,384,4096]{2,1,0:T(8,128)(2,1)} %down_hbm.1), custom_call_target="tpu_custom_call" | custom-call | tf_op jit(solution)/shard_map/pallas_call | solution.py:635
  109.4 0.7 copy.9

commit v4 on v3

--- a/solution.py
+++ b/solution.py
@@ -13,44 +13,42 @@
 F32 = jnp.float32
 
 
-D_COUNT = 2
 ORDERS = {
     4: [
-        "B0ab A1a C0ab A1b",
-        "B1a U0 V0 A2a",
-        "B1b A2b C1a B2a",
-        "C1b A3a B2b U1",
-        "A3b V1 B3a C2a",
-        "B3b C2b A4ab U2",
-        "V2 B4a C3a B4b",
-        "C3b U3 V3 C4ab",
-        "F3ba G3c U4 V4",
-        "F4ba G4c F2ba G2c",
-        "G3b G3a H4c G4b",
-        "G4a F1ba G1c H3c",
-        "H4b H4a H3b H3a",
-        "G2b G2a F0ba G0c",
-        "H2c H2b H2a G1b",
-        "H1c G1a H1b H1a",
-        "H0c G0b G0a H0b",
-        "H0a L0",
+        "B0a A1a B0b C0",
+        "A1b B1a U0 V0",
+        "A2a B1b C1 A2b",
+        "B2a U1 A3a V1",
+        "A3b B2b B3a C2",
+        "A4ab B3b U2 V2",
+        "B4a C3 B4b U3",
+        "V3 C4 F3ba G3c",
+        "U4 V4 F4ba G4c",
+        "F2ba G2c G3b G3a",
+        "H4c G4b G4a F1ba",
+        "G1c H3c H4b H4a",
+        "H3b H3a G2b G2a",
+        "F0ba G0c H2c H2b",
+        "H2a G1b H1c G1a",
+        "H1b H1a H0c G0b",
+        "G0a H0b H0a L0",
     ],
     1: [
-        "B0ab A1ab B1ab C0ab",
-        "U0 V0 C1ab U1",
+        "B0ab A1ab B1ab C0",
+        "U0 V0 C1 U1",
         "V1 F0ba G0c F1ba",
         "G1c G1ba H1cba G0ba",
         "H0cba L0",
     ],
     2: [
-        "B0ab A1a C0ab A1b",
+        "B0ab A1a C0 A1b",
         "B1a U0 V0 A2a",
-        "B1b A2b C1a B2a",
-        "C1b B2b U1 V1",
-        "C2ab F1ba G1c U2",
-        "V2 F2ba G2c F0ba",
-        "G0c G1ba G2ba H2cba",
-        "H1cba G0ba H0cba L0",
+        "B1b A2b C1 B2a",
+        "B2b U1 V1 C2",
+        "F1ba G1c U2 V2",
+        "F2ba G2c F0ba G0c",
+        "G1ba G2ba H2cba H1cba",
+        "G0ba H0cba L0",
     ],
 }
 
@@ -60,7 +58,6 @@
     nz,
     d_early,
     r_early,
-    d_count,
     order,
     tok_hbm,
     ids_ref,
@@ -104,14 +101,10 @@
     sel_send,
     sel_recv,
     sx_recv,
-    cx_send,
-    cx_recv,
     t_send,
     t_recv,
-    c1_send,
-    c1_recv,
-    c2_send,
-    c2_recv,
+    c_send,
+    c_recv,
     ce_send,
     ce_recv,
     tt_send,
@@ -130,23 +123,18 @@
     yl = tensor // 2
     half = nz // 2
     tok, width = tok_hbm.shape
-    def split(count, early):
-        full = width + early
-        cuts = [full * i // (128 * count) * 128 for i in range(count)]
-        whole = [pl.ds(a, b - a) for a, b in zip(cuts, cuts[1:] + [full])]
-        owns = [pl.ds(a, b - a) for a, b in zip(cuts, cuts[1:] + [width])]
-        starts = [early] + cuts[1:]
-        lates = [pl.ds(a, b - a) for a, b in zip(starts, cuts[1:] + [width])]
-        return whole, owns, lates
-
-    d_whole, d_owns, d_lates = split(d_count, d_early)
+    late_d = width - d_early
+    d_whole = (pl.ds(0, late_d), pl.ds(late_d, 2 * d_early))
+    own_late = pl.ds(0, late_d)
+    own_head = pl.ds(late_d, d_early)
+    extra = pl.ds(width, d_early)
+    head = pl.ds(0, d_early)
+    tail = pl.ds(d_early, late_d)
     late = width - r_early
     mid = late // 256 * 128
     r_count = 3
     r_whole = (pl.ds(0, mid), pl.ds(mid, late - mid), pl.ds(late, 2 * r_early))
     r_lates = (pl.ds(r_early, mid), pl.ds(r_early + mid, late - mid))
-    extra = pl.ds(width, d_early)
-    head = pl.ds(0, d_early)
     r_head = pl.ds(0, r_early)
 
     def side(piece, count):
@@ -187,8 +175,12 @@
     def wait_bytes(ref, sem):
         pltpu.make_async_copy(ref, ref, sem).wait()
 
-    tok_load = pltpu.make_async_copy(tok_hbm, tokx.at[:, pl.ds(0, width)], tok_sem)
-    tok_load.start()
+    tok_loads = (
+        pltpu.make_async_copy(tok_hbm.at[:, tail], tokx.at[:, own_late], tok_sem.at[0]),
+        pltpu.make_async_copy(tok_hbm.at[:, head], tokx.at[:, own_head], tok_sem.at[1]),
+    )
+    for load in tok_loads:
+        load.start()
     loads = []
     for q in range(4):
         rows = pl.ds(q * width, width)
@@ -253,7 +245,7 @@
         )
 
     def z_parts(s, piece):
-        return [z_copy(s, way, piece) for way in range(2) if s < half or way == side(piece, d_count)]
+        return [z_copy(s, way, piece) for way in range(2) if s < half or way == side(piece, 2)]
 
     def z_send(s, piece):
         start_all(z_parts(s, piece))
@@ -304,26 +296,27 @@
                 ).start()
 
     def send_piece(s, piece):
-        cols = d_owns[piece]
-        to_plane(
-            s, cols, own_q, cols, lambda r: sel_send.at[r], lambda r: sel_recv.at[s, r, piece]
-        )
-        if piece == d_count - 1:
-            to_plane(s, extra, far_q, head, lambda r: sel_send.at[r], lambda r: sx_recv.at[s, r])
+        send = lambda r: sel_send.at[r]
+        if piece == 0:
+            to_plane(s, own_late, own_q, tail, send, lambda r: sel_recv.at[s, r, 0])
+        else:
+            to_plane(s, own_head, own_q, head, send, lambda r: sel_recv.at[s, r, 1])
+            to_plane(s, extra, far_q, head, send, lambda r: sx_recv.at[s, r])
 
     routing(0)
-    tok_load.wait()
+    for load in tok_loads:
+        load.wait()
     pick_rows(0, d_whole[0])
     pl.semaphore_wait(barrier, len(peers))
 
-    e_copy = remote(tokx.at[:, head], tokx.at[:, extra], e_send, e_recv, t_peer)
+    e_copy = remote(tokx.at[:, own_head], tokx.at[:, extra], e_send, e_recv, t_peer)
     start_all([e_copy])
     z_send(1, 0)
     send_piece(0, 0)
     for d in range(1, nz):
         meta_copy(d).start()
-    for piece in range(1, d_count):
-        if piece == d_count - 1:
+    for piece in range(1, 2):
+        if piece == 2 - 1:
             e_copy.wait_recv()
         z_send(1, piece)
         pick_rows(0, d_whole[piece])
@@ -342,41 +335,38 @@
             pick_rows(b, d_whole[piece])
         send_piece(s, piece)
 
-    def t_copies(s, piece):
+    def t_copies(s):
         bl = pl.ds(*blocks(s))
         out = []
         for rel in range(2):
-            ref = xb.at[own_q if rel == 0 else far_q, rel, bl, :, d_lates[piece]]
-            out.append(remote(ref, ref, t_send, t_recv.at[s, rel, piece], t_peer))
+            ref = xb.at[own_q if rel == 0 else far_q, rel, bl, :, tail]
+            out.append(remote(ref, ref, t_send, t_recv.at[s, rel], t_peer))
         return out
 
-    def c_copies(s, piece, part):
-        bl = pl.ds(*blocks(s))
-        send, recv = ((c1_send, c1_recv), (cx_send, cx_recv), (c2_send, c2_recv))[part]
-        cols = (d_owns[piece], head, d_lates[piece])[part]
+    def c_copies(s, part):
+        bl = pl.ds(*blocks(s))
+        cols = (tail, head, head, tail)[part]
         out = []
         for rel in range(2):
-            ref = xb.at[own_q if (rel == 0) == (part == 0) else far_q, rel, bl, :, cols]
-            i = (s, rel) if part == 1 else (s, rel, piece)
-            out.append(remote(ref, ref, send, recv.at[i], c_peer))
+            ref = xb.at[own_q if (rel == 0) == (part < 2) else far_q, rel, bl, :, cols]
+            out.append(remote(ref, ref, c_send.at[part], c_recv.at[s, rel, part], c_peer))
         return out
 
     def stage_b(s, piece):
         bl = pl.ds(*blocks(s))
-        t_list, c_list = t_copies(s, piece), c_copies(s, piece, 0)
-        for rel in range(2):
-            got = xb.at[own_q if rel == 0 else far_q, rel, bl, :, d_owns[piece]]
-            wait_bytes(got, sel_recv.at[s, rel, piece])
-            start_all([t_list[rel], c_list[rel]])
-        if piece == d_count - 1:
-            x_list = c_copies(s, piece, 1)
-            for rel in range(2):
-                got = xb.at[far_q if rel == 0 else own_q, rel, bl, :, head]
-                wait_bytes(got, sx_recv.at[s, rel])
-                start_all([x_list[rel]])
-
-    def stage_c(s, piece):
-        t_list, c_list = t_copies(s, piece), c_copies(s, piece, 2)
+        for rel in range(2):
+            near, far = (own_q, far_q) if rel == 0 else (far_q, own_q)
+            cols = (tail, head)[piece]
+            wait_bytes(xb.at[near, rel, bl, :, cols], sel_recv.at[s, rel, piece])
+            if piece == 0:
+                start_all([t_copies(s)[rel], c_copies(s, 0)[rel]])
+            else:
+                start_all([c_copies(s, 1)[rel]])
+                wait_bytes(xb.at[far, rel, bl, :, head], sx_recv.at[s, rel])
+                start_all([c_copies(s, 2)[rel]])
+
+    def stage_c(s):
+        t_list, c_list = t_copies(s), c_copies(s, 3)
         for rel in range(2):
             t_list[rel].wait_recv()
             start_all([c_list[rel]])
@@ -400,11 +390,9 @@
         first, count = blocks(s)
         bl = pl.ds(first, count)
         rows = count * seat
-        for part in range(3):
-            for piece in range(d_count):
-                if part != 1 or piece == d_count - 1:
-                    for copy in c_copies(s, piece, part):
-                        copy.wait_recv()
+        for part in range(4):
+            for copy in c_copies(s, part):
+                copy.wait_recv()
         if not loaded["w1"]:
             loaded["w1"] = True
             for load in loads:
@@ -549,12 +537,10 @@
     for ref, sem in ((sel, sel_send), (ys, r_send)):
         wait_bytes(ref.at[0, :, some, :], sem.at[0])
         wait_bytes(ref.at[1], sem.at[1])
-    crossed = xb.at[0, :, :, :, pl.ds(d_early, width - d_early)]
-    wait_bytes(crossed, t_send)
-    wait_bytes(crossed, c2_send)
+    wait_bytes(xb.at[0, :, :, :, tail], t_send)
     wait_bytes(ts, tt_send)
-    wait_bytes(xb.at[0], c1_send)
-    wait_bytes(xb.at[0, :, :, :, head], cx_send)
+    for part, cols in enumerate((tail, head, head, tail)):
+        wait_bytes(xb.at[0, :, :, :, cols], c_send.at[part])
     wait_bytes(cr, ce_send)
 
 
@@ -603,7 +589,7 @@
         pltpu.VMEM((tok, r_early), BF16),
         pltpu.VMEM((tok, r_early), BF16),
         dma((12,)),
-        dma,
+        dma((2,)),
         dma,
         dma,
         dma,
@@ -611,18 +597,14 @@
         dma,
         dma((nz,)),
         dma,
-        dma((2 * chunks, D_COUNT)),
+        dma((2 * chunks, 2)),
         dma((2,)),
-        dma((chunks, 2, D_COUNT)),
+        dma((chunks, 2, 2)),
         dma((chunks, 2)),
         dma,
         dma((chunks, 2)),
-        dma,
-        dma((chunks, 2, D_COUNT)),
-        dma,
-        dma((chunks, 2, D_COUNT)),
-        dma,
-        dma((chunks, 2, D_COUNT)),
+        dma((4,)),
+        dma((chunks, 2, 4)),
         dma,
         dma((chunks, 2)),
         dma,
@@ -633,7 +615,7 @@
         dma((2 * chunks, 3)),
     ]
     return pl.pallas_call(
-        functools.partial(kernel, nx, nz, d_early, r_early, D_COUNT, make_order(half)),
+        functools.partial(kernel, nx, nz, d_early, r_early, make_order(half)),
         out_shape=pltpu.VMEM((tok, width), BF16),
         in_specs=[hbm, vmem, vmem, vmem, hbm, hbm, hbm],
         out_specs=vmem,
@@ -651,7 +633,7 @@
     return moe(nx, nz, d_early, r_early, tokens, *routing, *expert_weights)
 
 
-def solution(mesh, nx=4, nz=8, d_early=128, r_early=256):
+def solution(mesh, nx=4, nz=8, d_early=256, r_early=256):
     in_specs = (
         P("expert", "tensor"),
         P("expert", None),

time: 110 us -> 110 us (level); the launches traced: 110 us -> 109 us
    pallas_call x1, Pallas kernels: 109 us -> 108 us  [moe(): pl.pallas_call(functools.partial(kernel, nx, nz, d_early, r_early, make_o...]
where the time goes in v4:
time: 110 us; the launch traced here: 109 us
  Pallas kernels  108 us (98%)
    pallas_call x1, Pallas kernels, moe(): pl.pallas_call(functools.partial(kernel, nx, nz, d_early, r_early, make_o...  108 us

profile of v4, /device:TPU:8, one launch (start us, length us, event | category | flops | bytes accessed | tf_op | source)
XLA Modules:
  0.0 108.7 jit_solution(4750433590956577560)
XLA Ops:
  0.0 108.0 %shard_map.73 = bf16[128,1024]{1,0:T(8,128)(2,1)S(1)} custom-call(bf16[128,1024]{1,0:T(8,128)(2,1)} %tok_hbm.1, s32[8,128]{1,0:T(8,128)} %bitcast.3, s32[8,128]{1,0:T(8,128)} %bitcast.4, s32[8,128]{1,0:T(8,128)} %bitcast.5, bf16[1,4096,384]{2,1,0:T(8,128)(2,1)} %gate_hbm.1, bf16[1,4096,384]{2,1,0:T(8,128)(2,1)} %up_hbm.1, bf16[1,384,4096]{2,1,0:T(8,128)(2,1)} %down_hbm.1), custom_call_target="tpu_custom_call" | custom-call | tf_op jit(solution)/shard_map/pallas_call | solution.py:617
  108.0 0.7 copy.9
